TPU v7x, 128 devices: a whole 4x4x4 slice. The times are simulated.
128 devices in a mesh: dp: 4 (over y), expert: 32 (over x, z, core).
Axes of the slice: x: 4, y: 4, z: 4, core: 2. Of those that a mesh axis runs over, the one named last changes fastest.
Arguments:
- tokens: bfloat16 [262144, 3584], P(('dp', 'expert'))
- grads_out: bfloat16 [262144, 1024], P(('dp', 'expert')), may hold values from -0.0625 to 0.0625
- counts: int32 [128, 2], P(('dp', 'expert')), may hold values from 1 to 1920, as said below
- placement: int32 [32], replicated, may hold values from 0 to 31, as said below
- limits: float32 [32], P('expert'), may hold values from 0.3 to 1.5
Outputs:
- clipped: bfloat16 [32, 3584, 1024], P('expert', 'dp')
Inputs may be any that keep to these rules, and one draw needn't show every extreme that they name: For every device, the two counts rounded up to multiples of 128 sum to exactly 2048. Expert c's own slot is on expert index c; the redundant slot on expert index e copies expert placement[e]. An expert may have several copies or none.
All inputs are finite; a program needn't handle non-finite values.
Results may differ from a plain program's by a relative error of at most 0.015.
Values may be sent and summed in bfloat16 or wider, within the bound.
A program may use at most 128 MiB of HBM per device.

v0:
```python
import math

import jax
import jax.numpy as jnp
from jax import lax
from jax.sharding import PartitionSpec as P

BLOCK = 128


def local(tokens, grads_out, counts, placement, limits):
    row_count = tokens.shape[0]
    feature_width = tokens.shape[1]
    hidden_width = grads_out.shape[1]
    expert_count = lax.axis_size("expert")
    replica_count = lax.axis_size("dp")
    block_rows = feature_width // (replica_count * expert_count)
    first_count = counts[0, 0]
    second_count = counts[0, 1]
    padded_first = (first_count + BLOCK - 1) // BLOCK * BLOCK
    position = jnp.arange(row_count, dtype=jnp.int32)
    keep_first = (position < first_count).astype(grads_out.dtype)[:, None]
    keep_second = ((position >= padded_first) & (position < padded_first + second_count)).astype(
        grads_out.dtype
    )[:, None]
    masked = jnp.concatenate([grads_out * keep_first, grads_out * keep_second], axis=1)
    grouped = lax.dot_general(
        tokens, masked, (((0,), (0,)), ((), ())), preferred_element_type=jnp.float32
    )
    partial_value = grouped.astype(jnp.bfloat16).reshape(feature_width, 2, hidden_width)
    experts_range = jnp.arange(expert_count, dtype=jnp.int32)
    owners = (placement[None, :] == experts_range[:, None]).astype(jnp.bfloat16)
    spread = partial_value.reshape(1, replica_count, expert_count, block_rows, 2, hidden_width)
    arrived = lax.all_to_all(spread, "expert", split_axis=2, concat_axis=0, tiled=True)
    arrived = arrived.reshape(expert_count, replica_count, block_rows, 2, hidden_width)
    copies = jnp.einsum(
        "cs,sqrf->cqrf", owners, arrived[:, :, :, 1, :], preferred_element_type=jnp.float32
    )
    merged = arrived[:, :, :, 0, :].astype(jnp.float32) + copies
    reduced = lax.psum_scatter(
        merged.astype(jnp.bfloat16), "dp", scatter_dimension=1, tiled=True
    ).astype(jnp.float32)
    combined = reduced.reshape(expert_count, block_rows, hidden_width)
    owned_shard = lax.all_to_all(
        combined.astype(jnp.bfloat16), "expert", split_axis=0, concat_axis=1, tiled=True
    ).astype(combined.dtype)
    square_sum = lax.psum(jnp.sum(owned_shard * owned_shard), "dp")
    threshold = limits[0] * math.sqrt(feature_width * hidden_width)
    factor = jnp.minimum(1.0, threshold / jnp.sqrt(square_sum + 1e-06))
    return (owned_shard * factor).astype(jnp.bfloat16)


def solution(mesh):
    in_specs = (
        P(("dp", "expert"), None),
        P(("dp", "expert"), None),
        P(("dp", "expert"), None),
        P(),
        P("expert"),
    )
    out_specs = P("expert", "dp", None)
    return jax.shard_map(local, mesh=mesh, in_specs=in_specs, out_specs=out_specs, check_vma=False)
```

profile of v0, /device:TPU:0, one launch (start us, length us, event | category | flops | bytes accessed | tf_op | source)
XLA Modules:
  0.0 455.4 jit_solution(15023724612210397914)
XLA Ops:
  6.5 0.0 reduce-scatter.2.cloned.1.call-start
  6.5 1.3 fusion.14
  9.1 0.6 fusion.10
  9.7 2.6 broadcast_multiply_fusion.1
  12.3 36.8 %fusion.1 = bf16[3584,2048]{0,1:T(8,128)(2,1)} fusion(bf16[2048,3584]{1,0:T(8,128)(2,1)} %param.5, bf16[2048,1024]{1,0:T(8,128)(2,1)S(1)} %get-tuple-element.6, bf16[2048,1024]{1,0:T(8,128)(2,1)S(1)} %get-tuple-element.5), kind=kOutput, calls=%fused_computation.4 | convolution fusion | flops 30088888320 | bytes 37748736 | tf_op jit(solution)/shard_map/dot_general | solution.py:27
  49.0 20.3 %copy.14 = bf16[3584,2048]{1,0:T(8,128)(2,1)} copy(bf16[3584,2048]{0,1:T(8,128)(2,1)} %fusion.1) | data formatting | bytes 29360128 | tf_op jit(solution)/shard_map/convert_element_type | solution.py:30
  69.4 24.5 %reshape_reshape.3 = bf16[1,4,32,28,2,1024]{5,4,3,2,1,0:T(2,128)(2,1)} reshape(bf16[3584,2048]{1,0:T(8,128)(2,1)} %copy.14) | data formatting | bytes 29360128 | tf_op jit(solution)/shard_map/reshape;reshape | solution.py:33
  93.9 31.3 %copy.15 = bf16[1,4,32,28,2,1024]{5,1,4,3,0,2:T(4,128)(2,1)S(1)} copy(bf16[1,4,32,28,2,1024]{5,4,3,2,1,0:T(2,128)(2,1)} %reshape_reshape.3) | data formatting | bytes 29360128 | tf_op jit(solution)/shard_map/reshape;reshape | solution.py:33
  125.2 170.9 %all_to_all.24 = bf16[1,4,32,28,2,1024]{5,1,4,3,0,2:T(4,128)(2,1)S(1)} all-to-all(bf16[1,4,32,28,2,1024]{5,1,4,3,0,2:T(4,128)(2,1)S(1)} %copy.15), channel_id=1, replica_groups=mesh['dp'=4,'expert'=32] {'expert'}, dimensions={2} | all-to-all | bytes 29360128 | tf_op jit(solution)/shard_map/all_to_all | solution.py:34
  296.1 0.0 copy-start
  296.1 20.2 %copy.20 = bf16[1,4,32,28,2,1024]{5,2,3,1,4,0:T(8,128)(2,1)S(1)} copy(bf16[1,4,32,28,2,1024]{5,1,4,3,0,2:T(4,128)(2,1)S(1)} %all_to_all.24) | data formatting | bytes 29360128 | tf_op jit(solution)/shard_map/all_to_all | solution.py:34
  316.3 0.0 copy-done
  316.3 4.2 fusion
  320.5 0.0 reduce-scatter.2.cloned.1.call-update
  320.5 71.0 %reduce-scatter.2.cloned.1.call-done = bf16[32,1,28,1024]{3,0,2,1:T(8,128)(2,1)} async-done(((bf16[32,4,28,1024]{3,0,2,1:T(8,128)(2,1)}), bf16[32,1,28,1024]{3,0,2,1:T(8,128)(2,1)}) %reduce-scatter.2.cloned.1.call-update) | async-done | bytes 1835024 | tf_op jit(solution)/shard_map/reduce_scatter | solution.py:40
  391.5 3.9 copy.17
  395.3 7.2 %all-to-all-start.1 = ((bf16[32,28,1024]{2,1,0:T(8,128)(2,1)}), bf16[32,28,1024]{2,1,0:T(8,128)(2,1)S(1)}, u32[]{:S(2)}, u32[]{:S(2)}) async-start(bf16[32,28,1024]{2,1,0:T(8,128)(2,1)} %copy.17), calls=%async_computation.2 | async-start | bytes 4194304 | tf_op jit(solution)/shard_map/all_to_all | solution.py:44
  403.2 28.3 %all-to-all-done.1 = bf16[32,28,1024]{2,1,0:T(8,128)(2,1)S(1)} async-done(((bf16[32,28,1024]{2,1,0:T(8,128)(2,1)}), bf16[32,28,1024]{2,1,0:T(8,128)(2,1)S(1)}, u32[]{:S(2)}, u32[]{:S(2)}) %all-to-all-start.1) | async-done | bytes 1835040 | tf_op jit(solution)/shard_map/all_to_all | solution.py:44
  431.5 1.7 fusion.5
  433.2 9.2 %psum.7 = f32[]{:T(128)} all-reduce(f32[]{:T(128)} %fusion.5), channel_id=1, replica_groups=mesh['dp'=4,'expert'=32] {'dp'}, use_global_device_ids=true, to_apply=%region_2.3 | all-reduce | flops 1 | bytes 8 | tf_op jit(solution)/shard_map/psum | solution.py:47
  443.0 1.9 fusion.6
  444.9 3.7 convert_element_type.74
Async XLA Ops:
  6.5 384.9 %reduce-scatter.2.cloned.1.call-start = ((), (), s32[]{:S(2)}) async-start(), calls=%async_computation.3 | async-start | bytes 9175040 | tf_op jit(solution)/shard_map/reduce_scatter | solution.py:40
  296.1 20.2 %copy-start = (s32[32]{0:T(128)S(1)}, s32[32]{0:T(128)}, u32[]{:S(2)}) copy-start(s32[32]{0:T(128)} %param.8) | copy-start | bytes 388
  395.3 36.2 %all-to-all-start.1 = ((bf16[32,28,1024]{2,1,0:T(8,128)(2,1)}), bf16[32,28,1024]{2,1,0:T(8,128)(2,1)S(1)}, u32[]{:S(2)}, u32[]{:S(2)}) async-start(bf16[32,28,1024]{2,1,0:T(8,128)(2,1)} %copy.17), calls=%async_computation.2 | async-start | bytes 4194304 | tf_op jit(solution)/shard_map/all_to_all | solution.py:44
Sparse Core Ops, SparseCore 0:
  320.6 70.7 reduce-scatter.1
where the time goes:
time: 457 us; the launch traced here: 455 us
  blocking collectives  180 us (39%)
  local copies, waits for them, and re-layouts  105 us (23%)
  waiting for transfers between devices  99.3 us (22%)
  matrix products  41 us (9%)
  between operations  15.9 us (3%)
  starting transfers between devices  7.23 us (2%)
  other arithmetic  6.75 us (1%)
    all_to_all x1, blocking collectives, local(): lax.all_to_all(spread, 'expert', split_axis=2, concat_axis=0, tiled=True)  171 us
    reduce_scatter x1, waiting for transfers between devices, local(): lax.psum_scatter(merged.astype(jnp.bfloat16), 'dp', scatter_dimension=1,...  71 us
    another operation x2, local copies, waits for them, and re-layouts, local(): partial_value.reshape(1, replica_count, expert_count, block_rows, 2, hidd...  55.8 us
    dot_general x1, matrix products, local(): lax.dot_general(tokens, masked, (((0,), (0,)), ((), ())), preferred_eleme...  36.8 us
    all_to_all x1, waiting for transfers between devices, local(): lax.all_to_all(combined.astype(jnp.bfloat16), 'expert', split_axis=0, con...  28.3 us
    convert_element_type x1, local copies, waits for them, and re-layouts, local(): grouped.astype(jnp.bfloat16).reshape(feature_width, 2, hidden_width)  20.3 us
    all_to_all x1, local copies, waits for them, and re-layouts, local(): lax.all_to_all(spread, 'expert', split_axis=2, concat_axis=0, tiled=True)  20.2 us
    psum x1, blocking collectives, local(): square_sum = lax.psum(jnp.sum(owned_shard * owned_shard), 'dp')  9.21 us
  transfers between devices with their start and end apart: 2, of which 2 were waited for; matrix products, arithmetic and copies ran while one was open for 0% of the time, Pallas kernels for 0%

commit v1 on v0

v1 whole, which is shorter than its diff:
```python
import functools
import math

import jax
import jax.numpy as jnp
from jax import lax
from jax.experimental import pallas as pl
from jax.experimental.pallas import tpu as pltpu
from jax.sharding import PartitionSpec as P

MESH = pl.DeviceIdType.MESH
BF = jnp.bfloat16
F32 = jnp.float32

DP = 4
EX = 32
ROWS = 2048
DW = 3584
FW = 1024
HW = FW // 2
CH = 128
NJ = DW // DP // CH
ND = 2
NA = NJ - ND
NU = 2 * NA + ND
NX = 3

FIRST = [(0, 1), (1, 1), (NA, 1), (2, 1), (NA + 1, 1), (3, 1), (4, 1)]
SECOND = [(j, 0) for j in range(NJ)]


def unit(j, s):
    return j if s == 1 else NA + j


def body(
    x_ref, g_ref, counts_ref, place_ref, limit_ref, out_ref, factor_ref,
    xc, G, Pb, H1, H2, d_in, d_mid, d_back, S1, a_in, a_mid, a_back, CD, CA,
    T, acc, norms, tab_v, tab_s,
    x_sem, g_sem, tab_sem, y_send, h1_sem, h2_sem, a2a_send, a2a_recv, own_sem,
    n_send, n_recv, out_sem,
):
    d = lax.axis_index("dp")
    e = lax.axis_index("expert")
    up = lax.rem(d + 1, DP)
    dn = lax.rem(d + 3, DP)
    opp = lax.rem(d + 2, DP)
    ex = e // 8
    ez = lax.rem(e // 2, 4)
    ec = lax.rem(e, 2)
    turn = 1 - 2 * ec

    def peer(i):
        px = lax.rem(ex + turn * (i // 8) + 4, 4)
        pz = lax.rem(ez + turn * lax.rem(i // 2, 4) + 4, 4)
        pc = lax.rem(ec + lax.rem(i, 2), 2)
        return (px * 4 + pz) * 2 + pc

    def g_load(s):
        return pltpu.make_async_copy(g_ref, G.at[:, pl.ds(s * FW, FW)], g_sem.at[s])

    def x_load(i, j):
        return [
            pltpu.make_async_copy(
                x_ref.at[:, pl.ds(t * (DW // DP) + j * CH, CH)],
                xc.at[i % NX, :, pl.ds(t * CH, CH)],
                x_sem.at[(i % NX) * 4 + t],
            )
            for t in range(4)
        ]

    steps = FIRST + SECOND
    g_load(1).start()
    for i in range(NX - 1):
        for c in x_load(i, steps[i][0]):
            c.start()
    g_load(0).start()

    bar = pltpu.get_barrier_semaphore()
    for k in range(1, DP):
        pl.semaphore_signal(
            bar, inc=1, device_id=(lax.rem(d + k, DP), e), device_id_type=MESH
        )

    def greet(k, c):
        pl.semaphore_signal(
            bar, inc=1, device_id=(d, lax.rem(e + k, EX)), device_id_type=MESH
        )
        return c

    lax.fori_loop(1, EX, greet, 0)

    row = place_ref[...]
    ri = lax.broadcasted_iota(jnp.int32, (EX, EX), 0)
    ci = lax.broadcasted_iota(jnp.int32, (EX, EX), 1)
    across = jnp.broadcast_to(row, (EX, EX))
    down = jnp.sum(jnp.where(ri == ci, across, 0), axis=1, keepdims=True)
    tab_v[0:1, 0:EX] = jnp.max(
        jnp.where((down == across) & (ri < ci), ri + 1, 0), axis=0, keepdims=True
    )
    tab_v[1:2, 0:EX] = jnp.max(
        jnp.where(down == ci, ri + 1, 0), axis=0, keepdims=True
    )
    tab = pltpu.make_async_copy(tab_v, tab_s, tab_sem)
    tab.start()

    first = counts_ref[0, 0]
    second = counts_ref[0, 1]
    padded = (first + 127) // 128 * 128

    def mask(s):
        g_load(s).wait()
        lo = padded if s == 1 else 0
        hi = padded + second if s == 1 else first

        @pl.loop(0, ROWS // 128)
        def _(b):
            r = pl.ds(pl.multiple_of(b * 128, 128), 128)
            pos = lax.broadcasted_iota(jnp.int32, (128, FW), 0) + b * 128
            g = G[r, pl.ds(s * FW, FW)]
            G[r, pl.ds(s * FW, FW)] = jnp.where(
                (pos >= lo) & (pos < hi), g, jnp.zeros_like(g)
            )

    state = {"i": 0}

    def compute(j, s):
        i = state["i"]
        state["i"] = i + 1
        assert steps[i] == (j, s)
        n = i + NX - 1
        if n < len(steps):
            for c in x_load(n, steps[n][0]):
                c.start()
        for c in x_load(i, j):
            c.wait()

        @pl.loop(0, FW // 512)
        def _(n):
            col = pl.ds(pl.multiple_of(s * FW + n * 512, 512), 512)
            r = lax.dot_general(
                xc[i % NX],
                G[:, col],
                (((0,), (0,)), ((), ())),
                preferred_element_type=F32,
            )
            Pb[j, :, :, col] = r.astype(BF).reshape(4, CH, 512)

    def y_copy(src, dst, u, sem, target):
        return pltpu.make_async_remote_copy(
            src, dst, y_send.at[u], sem, device_id=(target, e), device_id_type=MESH
        )

    def halves(s):
        return pl.ds(s * FW, HW), pl.ds(s * FW + HW, HW)

    left, right = pl.ds(0, HW), pl.ds(HW, HW)

    def raw(j, s):
        u = unit(j, s)
        ha, hb = halves(s)
        y_copy(Pb.at[j, opp, :, ha], H1.at[0, u], u, h1_sem.at[0, u], dn).start()
        y_copy(Pb.at[j, opp, :, hb], H1.at[1, u], u, h1_sem.at[1, u], up).start()
        y_copy(Pb.at[j, dn, :, hb], H2.at[0, u, :, right], u, h2_sem.at[0, u], dn).start()
        y_copy(Pb.at[j, up, :, ha], H2.at[1, u, :, left], u, h2_sem.at[1, u], up).start()

    def merge(j, s):
        u = unit(j, s)
        ha, hb = halves(s)
        for k, t, h, half in ((0, dn, ha, left), (1, up, hb, right)):
            pltpu.make_async_copy(H1.at[k, u], H1.at[k, u], h1_sem.at[k, u]).wait()

            @pl.loop(0, CH // 32)
            def _(b):
                r = pl.ds(pl.multiple_of(b * 32, 32), 32)
                v = Pb[j, t, r, h].astype(F32) + H1[k, u, r, :].astype(F32)
                Pb[j, t, r, h] = v.astype(BF)

            y_copy(
                Pb.at[j, t, :, h], H2.at[k, u, :, half], u, h2_sem.at[k, u], t
            ).start()

    def arrived(u):
        for k in range(2):
            pltpu.make_async_copy(H2.at[k, u], H2.at[k, u], h2_sem.at[k, u]).wait()

    def reduce_second(j):
        u = unit(j, 1)
        arrived(u)

        @pl.loop(0, CH // 16)
        def _(b):
            r = pl.ds(pl.multiple_of(b * 16, 16), 16)
            v = Pb[j, d, r, pl.ds(FW, FW)].astype(F32)
            v = v + H2[0, u, r, :].astype(F32) + H2[1, u, r, :].astype(F32)
            S1[j, r, :] = v.astype(BF)

    def exchange(a, src, dst):
        own = pltpu.make_async_copy(src(e), dst.at[e], own_sem.at[a])
        own.start()

        def send(i, c):
            p = peer(i)
            pltpu.make_async_remote_copy(
                src(p), dst.at[e], a2a_send.at[a], a2a_recv.at[a],
                device_id=(d, p), device_id_type=MESH,
            ).start()
            return c

        lax.fori_loop(1, EX, send, 0)
        return own

    def all_in(a, dst):
        pltpu.make_async_copy(
            dst.at[pl.ds(0, EX - 1)], dst.at[pl.ds(0, EX - 1)], a2a_recv.at[a]
        ).wait()

    def chain(inp, mid, C):
        C[0] = jnp.zeros(C.shape[1:], F32)

        def add(i, c):
            C[i + 1] = C[tab_s[0, i]] + inp[i].astype(F32)
            return c

        lax.fori_loop(0, EX, add, 0)

        def pick(i, c):
            mid[i] = C[tab_s[1, i]].astype(BF)
            return c

        lax.fori_loop(0, EX, pick, 0)

    owns = {}

    def d_route(k):
        j = NA + k

        def src(q):
            r = pl.ds(pl.multiple_of(lax.rem(q, 8) * 16, 16), 16)
            return Pb.at[j, q // 8, r, pl.ds(FW, FW)]

        owns[2 * k] = exchange(2 * k, src, d_in.at[k])

    def d_return(k):
        owns[2 * k].wait()
        all_in(2 * k, d_in.at[k])
        chain(d_in.at[k], d_mid.at[k], CD)
        owns[2 * k + 1] = exchange(2 * k + 1, lambda q: d_mid.at[k, q], d_back.at[k])

    def d_add(k):
        owns[2 * k + 1].wait()
        all_in(2 * k + 1, d_back.at[k])

        @pl.loop(0, EX)
        def _(q):
            t = q // 8
            r = pl.ds(pl.multiple_of(lax.rem(q, 8) * 16, 16), 16)
            v = Pb[NA + k, t, r, pl.ds(0, FW)].astype(F32) + d_back[k, q].astype(F32)
            Pb[NA + k, t, r, pl.ds(0, FW)] = v.astype(BF)

    A1, A2 = 2 * ND, 2 * ND + 1

    def a_route():
        def src(q):
            r = pl.ds(pl.multiple_of(q // 4 * 16, 16), 16)
            c = pl.ds(pl.multiple_of(lax.rem(q, 4) * 256, 256), 256)
            return S1.at[:, r, c]

        owns[A1] = exchange(A1, src, a_in)

    def a_return():
        owns[A1].wait()
        all_in(A1, a_in)
        chain(a_in, a_mid, CA)
        owns[A2] = exchange(A2, lambda q: a_mid.at[q], a_back)

    def a_ready():
        owns[A2].wait()
        all_in(A2, a_back)

    def total(j):
        u = unit(j, 0)
        arrived(u)

        @pl.loop(0, CH // 16)
        def _(b):
            r = pl.ds(pl.multiple_of(b * 16, 16), 16)
            for c in range(4):
                col = pl.ds(c * 256, 256)
                v = Pb[j, d, r, col].astype(F32)
                v = v + H2[0, u, r, col].astype(F32) + H2[1, u, r, col].astype(F32)
                if j < NA:
                    v = v + a_back[b * 4 + c, j].astype(F32)
                w = v * v
                acc[:, col] += w[0:8] + w[8:16]
                T[j, r, col] = v.astype(BF)

        out_copy(j).start()

    def out_copy(j):
        return pltpu.make_async_copy(
            T.at[j], out_ref.at[pl.ds(j * CH, CH), :], out_sem.at[j]
        )

    acc[...] = jnp.zeros_like(acc)
    mask(1)
    compute(0, 1)
    pl.semaphore_wait(bar, EX - 1 + DP - 1)
    raw(0, 1)
    compute(1, 1)
    raw(1, 1)
    compute(NA, 1)
    d_route(0)
    merge(0, 1)
    compute(2, 1)
    raw(2, 1)
    compute(NA + 1, 1)
    d_route(1)
    merge(1, 1)
    compute(3, 1)
    raw(3, 1)
    tab.wait()
    mask(0)
    merge(2, 1)
    compute(4, 1)
    raw(4, 1)
    d_return(0)
    merge(3, 1)
    compute(0, 0)
    compute(1, 0)
    merge(4, 1)
    raw(0, 0)
    raw(1, 0)
    d_return(1)
    compute(2, 0)
    raw(2, 0)
    merge(0, 0)
    compute(3, 0)
    raw(3, 0)
    compute(4, 0)
    for j in range(NA):
        reduce_second(j)
    a_route()
    raw(4, 0)
    compute(NA, 0)
    compute(NA + 1, 0)
    merge(1, 0)
    d_add(0)
    raw(NA, 0)
    merge(2, 0)
    d_add(1)
    raw(NA + 1, 0)
    merge(3, 0)
    a_return()
    merge(4, 0)
    merge(NA, 0)
    merge(NA + 1, 0)
    a_ready()
    for j in range(NJ):
        total(j)

    square = jnp.sum(acc[...])
    norms[d] = jnp.full((8, 128), square, F32)
    for k in range(1, DP):
        pltpu.make_async_remote_copy(
            norms.at[d], norms.at[d], n_send, n_recv,
            device_id=(lax.rem(d + k, DP), e), device_id_type=MESH,
        ).start()
    pltpu.make_async_copy(norms.at[pl.ds(0, 3)], norms.at[pl.ds(0, 3)], n_recv).wait()
    whole = norms[0] + norms[1] + norms[2] + norms[3]
    threshold = limit_ref[0] * math.sqrt(DW * FW)
    factor_ref[...] = jnp.minimum(1.0, threshold / jnp.sqrt(whole + 1e-06))

    pltpu.make_async_copy(norms.at[pl.ds(0, 3)], norms.at[pl.ds(0, 3)], n_send).wait()
    for u in range(NU):
        pltpu.make_async_copy(
            H2.at[0, pl.ds(0, 3)], H2.at[0, pl.ds(0, 3)], y_send.at[u]
        ).wait()
    for a in range(2 * ND + 2):
        ref = d_in.at[0] if a < 2 * ND else a_in
        pltpu.make_async_copy(
            ref.at[pl.ds(0, EX - 1)], ref.at[pl.ds(0, EX - 1)], a2a_send.at[a]
        ).wait()
    for j in range(NJ):
        out_copy(j).wait()


def local(tokens, grads_out, counts, placement, limits):
    dma = pltpu.SemaphoreType.DMA
    total, factor = pl.pallas_call(
        body,
        out_shape=(
            jax.ShapeDtypeStruct((DW // DP, FW), BF),
            jax.ShapeDtypeStruct((8, 128), F32),
        ),
        in_specs=[
            pl.BlockSpec(memory_space=pl.ANY),
            pl.BlockSpec(memory_space=pl.ANY),
            pl.BlockSpec(memory_space=pltpu.SMEM),
            pl.BlockSpec(memory_space=pltpu.VMEM),
            pl.BlockSpec(memory_space=pltpu.SMEM),
        ],
        out_specs=(
            pl.BlockSpec(memory_space=pl.ANY),
            pl.BlockSpec(memory_space=pltpu.VMEM),
        ),
        scratch_shapes=[
            pltpu.VMEM((NX, ROWS, 4 * CH), BF),
            pltpu.VMEM((ROWS, 2 * FW), BF),
            pltpu.VMEM((NJ, 4, CH, 2 * FW), BF),
            pltpu.VMEM((2, NU, CH, HW), BF),
            pltpu.VMEM((2, NU, CH, FW), BF),
            pltpu.VMEM((ND, EX, 16, FW), BF),
            pltpu.VMEM((ND, EX, 16, FW), BF),
            pltpu.VMEM((ND, EX, 16, FW), BF),
            pltpu.VMEM((NA, CH, FW), BF),
            pltpu.VMEM((EX, NA, 16, 256), BF),
            pltpu.VMEM((EX, NA, 16, 256), BF),
            pltpu.VMEM((EX, NA, 16, 256), BF),
            pltpu.VMEM((EX + 1, 16, FW), F32),
            pltpu.VMEM((EX + 1, NA, 16, 256), F32),
            pltpu.VMEM((NJ, CH, FW), BF),
            pltpu.VMEM((8, FW), F32),
            pltpu.VMEM((DP, 8, 128), F32),
            pltpu.VMEM((8, 128), jnp.int32),
            pltpu.SMEM((8, 128), jnp.int32),
            dma((NX * 4,)),
            dma((2,)),
            dma,
            dma((NU,)),
            dma((2, NU)),
            dma((2, NU)),
            dma((2 * ND + 2,)),
            dma((2 * ND + 2,)),
            dma((2 * ND + 2,)),
            dma,
            dma,
            dma((NJ,)),
        ],
        compiler_params=pltpu.CompilerParams(
            collective_id=0, has_side_effects=True, vmem_limit_bytes=62 * 2**20
        ),
        cost_estimate=pl.CostEstimate(
            flops=4 * ROWS * DW * FW, bytes_accessed=40 * 2**20, transcendentals=0
        ),
    )(tokens, grads_out, counts, placement.reshape(1, EX), limits)
    return (total.astype(F32) * factor[0, 0]).astype(BF)[None]


def solution(mesh):
    in_specs = (
        P(("dp", "expert"), None),
        P(("dp", "expert"), None),
        P(("dp", "expert"), None),
        P(),
        P("expert"),
    )
    out_specs = P("expert", "dp", None)
    return jax.shard_map(local, mesh=mesh, in_specs=in_specs, out_specs=out_specs, check_vma=False)
```

time: 457 us -> 124 us (0.27)
  blocking collectives: 180 us -> 0 us
  Pallas kernels: 0 us -> 118 us
  local copies, waits for them, and re-layouts: 105 us -> 1.26 us
  waiting for transfers between devices: 99.3 us -> 0 us
  matrix products: 41 us -> 0 us
  between operations: 15.9 us -> 0.66 us
  starting transfers between devices: 7.23 us -> 0 us
    all_to_all x1 -> x0, blocking collectives: 171 us -> none  [local(): lax.all_to_all(spread, 'expert', split_axis=2, concat_axis=0, tiled=True)]
    pallas_call x0 -> x1, Pallas kernels: none -> 118 us  [local(): pl.pallas_call(body, out_shape=(jax.ShapeDtypeStruct((DW // DP, FW), BF),...]
    reduce_scatter x1 -> x0, waiting for transfers between devices: 71 us -> none  [local(): lax.psum_scatter(merged.astype(jnp.bfloat16), 'dp', scatter_dimension=1,...]
    another operation x2 -> x0, local copies, waits for them, and re-layouts: 55.8 us -> none  [local(): partial_value.reshape(1, replica_count, expert_count, block_rows, 2, hidd...]
    dot_general x2 -> x0, matrix products: 41 us -> none  [the longest x1 36.8 us: local(): lax.dot_general(tokens, masked, (((0,), (0,)), ((), ())), preferred_eleme...]
    all_to_all x1 -> x0, waiting for transfers between devices: 28.3 us -> none  [local(): lax.all_to_all(combined.astype(jnp.bfloat16), 'expert', split_axis=0, con...]
    convert_element_type x3 -> x0, local copies, waits for them, and re-layouts: 27.9 us -> none  [the longest x1 20.3 us: local(): grouped.astype(jnp.bfloat16).reshape(feature_width, 2, hidden_width)]
    all_to_all x1 -> x0, local copies, waits for them, and re-layouts: 20.2 us -> none  [local(): lax.all_to_all(spread, 'expert', split_axis=2, concat_axis=0, tiled=True)]
  transfers between devices with their start and end apart: 2 -> 0, of which waited for: 2 -> 0; matrix products, arithmetic and copies ran while one was open for 0% -> 0% of each run, Pallas kernels for 0% -> 0%
where the time goes in v1:
time: 124 us; the launch traced here: 123 us
  Pallas kernels  118 us (95%)
  other arithmetic  3.85 us (3%)
  local copies, waits for them, and re-layouts  1.26 us (1%)
    pallas_call x1, Pallas kernels, local(): pl.pallas_call(body, out_shape=(jax.ShapeDtypeStruct((DW // DP, FW), BF),...  118 us
    broadcast_in_dim x1, other arithmetic, local(): return (total.astype(F32) * factor[0, 0]).astype(BF)[None]  3.85 us

profile of v1, /device:TPU:0, one launch (start us, length us, event | category | flops | bytes accessed | tf_op | source)
XLA Modules:
  0.0 123.4 jit_solution(1356281512266864642)
XLA Ops:
  0.7 117.6 %shard_map.55 = (bf16[896,1024]{1,0:T(8,128)(2,1)}, f32[8,128]{1,0:T(8,128)}) custom-call(bf16[2048,3584]{1,0:T(8,128)(2,1)} %x_ref.1, bf16[2048,1024]{1,0:T(8,128)(2,1)} %g_ref.1, s32[1,2]{1,0:T(1,128)} %counts_ref.1, s32[1,32]{1,0:T(1,128)} %bitcast.4, f32[1]{0:T(128)S(6)} %copy.6.limit_ref), custom_call_target="tpu_custom_call" | custom-call | flops 30064771072 | bytes 41943040 | tf_op jit(solution)/shard_map/pallas_call | solution.py:390
  118.3 1.3 %slice.3 = f32[1,1]{1,0:T(1,128)} slice(f32[8,128]{1,0:T(8,128)} %get-tuple-element.8), slice={[0:1], [0:1]} | slice | bytes 8 | tf_op jit(solution)/shard_map/slice | solution.py:447
  119.5 3.9 %fusion = bf16[1,896,1024]{2,1,0:T(8,128)(2,1)} fusion(bf16[896,1024]{1,0:T(8,128)(2,1)} %get-tuple-element.7, f32[]{:T(128)} %bitcast.1), kind=kLoop, calls=%fused_computation.1 | loop fusion | flops 2752512 | bytes 3670020 | tf_op jit(solution)/shard_map/broadcast_in_dim | solution.py:447

commit v2 on v1

v2 whole, which is shorter than its diff:
```python
import functools
import math

import jax
import jax.numpy as jnp
from jax import lax
from jax.experimental import pallas as pl
from jax.experimental.pallas import tpu as pltpu
from jax.sharding import PartitionSpec as P

MESH = pl.DeviceIdType.MESH
BF = jnp.bfloat16
F32 = jnp.float32

DP = 4
EX = 32
ROWS = 2048
DW = 3584
FW = 1024
HW = FW // 2
CH = 128
NJ = DW // DP // CH
ND = 3
NA = NJ - ND
NU = 2 * NA + ND
NG = NA // 2
NX = 3
PARTS = 4

START = ["c41", "c01"]
ORDER = [
    "c21", "w21", "h21", "c51", "dr1", "m01", "c11", "h11", "c31", "w31",
    "h31", "c00", "w00", "dret0", "h00", "m21", "c61", "m31", "c40", "dr2",
    "m00", "c30", "r0", "w11", "c10", "h10", "c20", "h20", "da0", "r3",
    "r2", "m11", "dret1", "h30", "w10", "w20", "h40", "c50", "m10", "c60",
    "dret2", "m30", "r1", "w30", "pre1", "m40", "ar0", "da1", "h50", "da2",
    "w50", "h60", "m20", "pre0", "ar1", "w60", "pre3", "aret0", "m60",
    "w40", "aret1", "m50", "ardy0", "tot4", "tot6", "pre2", "fin0", "fin1",
    "ardy1", "fin2", "fin3", "tot5",
]
STEPS = [(int(o[1]), int(o[2])) for o in START + ORDER if o[0] == "c"]


def unit(j, s):
    return j if s == 1 else NA + j


def body(
    x_ref, g_ref, counts_ref, place_ref, limit_ref, out_ref, norm_ref,
    xc, G, Pb, H1, H2, d_in, d_mid, d_back, S1, a_in, a_mid, a_back, CD, CA,
    T, acc, norm, tab_v, tab_s,
    z_sem, c_sem, x_sem, g_sem, tab_sem, y_send, h1_sem, h2_sem, a2a_send, a2a_recv, own_sem,
    n_send, n_recv, n_own, out_sem,
):
    d = lax.axis_index("dp")
    e = lax.axis_index("expert")
    up = lax.rem(d + 1, DP)
    dn = lax.rem(d + 3, DP)
    opp = lax.rem(d + 2, DP)
    ex = e // 8
    ez = lax.rem(e // 2, 4)
    ec = lax.rem(e, 2)
    turn = 1 - 2 * ec

    def peer(i):
        px = lax.rem(ex + turn * (i // 8) + 4, 4)
        pz = lax.rem(ez + turn * lax.rem(i, 4) + 4, 4)
        pc = lax.rem(ec + lax.rem(i // 4, 2), 2)
        return (px * 4 + pz) * 2 + pc

    def g_load(s, q):
        r = pl.ds(q * 512, 512)
        return pltpu.make_async_copy(
            g_ref.at[r, :], G.at[r, pl.ds(s * FW, FW)], g_sem.at[s * 4 + q]
        )

    def x_load(i, j):
        return [
            pltpu.make_async_copy(
                x_ref.at[:, pl.ds(t * (DW // DP) + j * CH, CH)],
                xc.at[i % NX, :, pl.ds(t * CH, CH)],
                x_sem.at[(i % NX) * 4 + t],
            )
            for t in range(4)
        ]

    steps = STEPS
    for q in range(4):
        g_load(1, q).start()
    for i in range(NX - 1):
        for c in x_load(i, steps[i][0]):
            c.start()
    for q in range(4):
        g_load(0, q).start()

    def at(kx, kz, kc):
        return (lax.rem(ex + kx, 4) * 4 + lax.rem(ez + kz, 4)) * 2 + lax.rem(ec + kc, 2)

    def signal(sem, td, te):
        pl.semaphore_signal(sem, inc=1, device_id=(td, te), device_id_type=MESH)

    bar = pltpu.get_barrier_semaphore()
    for k in range(1, 4):
        signal(bar, lax.rem(d + k, DP), e)
        signal(bar, d, at(k, 0, 0))
        signal(bar, d, at(0, k, 0))
    signal(bar, d, at(0, 0, 1))

    def greet_near():
        pl.semaphore_wait(bar, 10)
        for k in range(1, 4):
            signal(z_sem, d, at(0, k, 0))

    def greet_plane():
        pl.semaphore_wait(z_sem, 3)
        signal(c_sem, d, at(0, 0, 1))

    def plane_ready():
        pl.semaphore_wait(c_sem, 1)

    row = place_ref[...]
    ri = lax.broadcasted_iota(jnp.int32, (EX, EX), 0)
    ci = lax.broadcasted_iota(jnp.int32, (EX, EX), 1)
    across = jnp.broadcast_to(row, (EX, EX))
    down = jnp.sum(jnp.where(ri == ci, across, 0), axis=1, keepdims=True)
    tab_v[0:1, 0:EX] = jnp.max(
        jnp.where((down == across) & (ri < ci), ri + 1, 0), axis=0, keepdims=True
    )
    tab_v[1:2, 0:EX] = jnp.max(
        jnp.where(down == ci, ri + 1, 0), axis=0, keepdims=True
    )
    tab = pltpu.make_async_copy(tab_v, tab_s, tab_sem)
    tab.start()

    first = counts_ref[0, 0]
    second = counts_ref[0, 1]
    padded = (first + 127) // 128 * 128

    def mask(s):
        lo = padded if s == 1 else 0
        hi = padded + second if s == 1 else first
        for q in range(4):
            g_load(s, q).wait()

            @pl.loop(0, 4)
            def _(b):
                r = pl.ds(pl.multiple_of(q * 512 + b * 128, 128), 128)
                pos = lax.broadcasted_iota(jnp.int32, (128, FW), 0) + (q * 512 + b * 128)
                g = G[r, pl.ds(s * FW, FW)]
                G[r, pl.ds(s * FW, FW)] = jnp.where(
                    (pos >= lo) & (pos < hi), g, jnp.zeros_like(g)
                )

    def prefetch(n):
        if n < len(steps):
            for c in x_load(n, steps[n][0]):
                c.start()

    def half(i, n):
        j, s = steps[i]
        col = pl.ds(pl.multiple_of(s * FW + n * 512, 512), 512)
        r = lax.dot_general(
            xc[i % NX],
            G[:, col],
            (((0,), (0,)), ((), ())),
            preferred_element_type=F32,
        )
        Pb[j, :, :, col] = r.astype(BF).reshape(4, CH, 512)

    def x_wait(i):
        for c in x_load(i, steps[i][0]):
            c.wait()

    def compute(j, s):
        i = steps.index((j, s))
        prefetch(i + NX - 1)
        x_wait(i)
        pl.loop(0, 2)(functools.partial(half, i))

    def y_copy(src, dst, u, sem, target):
        return pltpu.make_async_remote_copy(
            src, dst, y_send.at[u], sem, device_id=(target, e), device_id_type=MESH
        )

    def halves(s):
        return pl.ds(s * FW, HW), pl.ds(s * FW + HW, HW)

    left, right = pl.ds(0, HW), pl.ds(HW, HW)

    def raw_left(j, s):
        u = unit(j, s)
        ha, hb = halves(s)
        y_copy(Pb.at[j, opp, :, ha], H1.at[0, u], u, h1_sem.at[0, u], dn).start()
        y_copy(Pb.at[j, up, :, ha], H2.at[1, u, :, left], u, h2_sem.at[1, u], up).start()

    def raw_right(j, s):
        u = unit(j, s)
        ha, hb = halves(s)
        y_copy(Pb.at[j, opp, :, hb], H1.at[1, u], u, h1_sem.at[1, u], up).start()
        y_copy(Pb.at[j, dn, :, hb], H2.at[0, u, :, right], u, h2_sem.at[0, u], dn).start()

    def first_hop(j, s):
        u = unit(j, s)
        ha, hb = halves(s)
        y_copy(Pb.at[j, opp, :, ha], H1.at[0, u], u, h1_sem.at[0, u], dn).start()
        y_copy(Pb.at[j, opp, :, hb], H1.at[1, u], u, h1_sem.at[1, u], up).start()

    def whole_hop(j, s):
        u = unit(j, s)
        ha, hb = halves(s)
        y_copy(Pb.at[j, dn, :, hb], H2.at[0, u, :, right], u, h2_sem.at[0, u], dn).start()
        y_copy(Pb.at[j, up, :, ha], H2.at[1, u, :, left], u, h2_sem.at[1, u], up).start()

    def merge(j, s):
        u = unit(j, s)
        ha, hb = halves(s)
        for k, t, h, half in ((0, dn, ha, left), (1, up, hb, right)):
            pltpu.make_async_copy(H1.at[k, u], H1.at[k, u], h1_sem.at[k, u]).wait()

            @pl.loop(0, CH // 32)
            def _(b):
                r = pl.ds(pl.multiple_of(b * 32, 32), 32)
                v = Pb[j, t, r, h].astype(F32) + H1[k, u, r, :].astype(F32)
                Pb[j, t, r, h] = v.astype(BF)

            y_copy(
                Pb.at[j, t, :, h], H2.at[k, u, :, half], u, h2_sem.at[k, u], t
            ).start()

    def arrived(u):
        for k in range(2):
            pltpu.make_async_copy(H2.at[k, u], H2.at[k, u], h2_sem.at[k, u]).wait()

    def reduce_second(j):
        u = unit(j, 1)
        arrived(u)

        @pl.loop(0, CH // 16)
        def _(b):
            r = pl.ds(pl.multiple_of(b * 16, 16), 16)
            v = Pb[j, d, r, pl.ds(FW, FW)].astype(F32)
            v = v + H2[0, u, r, :].astype(F32) + H2[1, u, r, :].astype(F32)
            S1[j, r, :] = v.astype(BF)

    def one(a, src, dst, p):
        pltpu.make_async_remote_copy(
            src(p), dst.at[e], a2a_send.at[a], a2a_recv.at[a],
            device_id=(d, p), device_id_type=MESH,
        ).start()

    def keep_own(a, src, dst):
        own = pltpu.make_async_copy(src(e), dst.at[e], own_sem.at[a])
        own.start()
        return own

    def exchange(a, src, dst):
        def send(i, c):
            one(a, src, dst, peer(i))
            return c

        lax.fori_loop(1, EX, send, 0)
        return keep_own(a, src, dst)

    def all_in(a, dst):
        pltpu.make_async_copy(
            dst.at[pl.ds(0, EX - 1)], dst.at[pl.ds(0, EX - 1)], a2a_recv.at[a]
        ).wait()

    def chain(inp, mid, C):
        C[0] = jnp.zeros(C.shape[1:], F32)

        def add(i, c):
            C[i + 1] = C[tab_s[0, i]] + inp[i].astype(F32)
            return c

        lax.fori_loop(0, EX, add, 0)

        def pick(i, c):
            mid[i] = C[tab_s[1, i]].astype(BF)
            return c

        lax.fori_loop(0, EX, pick, 0)

    owns = {}

    def d_src(k, q):
        r = pl.ds(pl.multiple_of(lax.rem(q, 8) * 16, 16), 16)
        return Pb.at[NA + k, q // 8, r, pl.ds(FW, FW)]

    def d_route(k):
        owns[2 * k] = exchange(2 * k, functools.partial(d_src, k), d_in.at[k])

    def d_return(k):
        owns[2 * k].wait()
        all_in(2 * k, d_in.at[k])
        chain(d_in.at[k], d_mid.at[k], CD)
        owns[2 * k + 1] = exchange(2 * k + 1, lambda q: d_mid.at[k, q], d_back.at[k])

    def d_add(k):
        owns[2 * k + 1].wait()
        all_in(2 * k + 1, d_back.at[k])

        @pl.loop(0, EX)
        def _(q):
            t = q // 8
            r = pl.ds(pl.multiple_of(lax.rem(q, 8) * 16, 16), 16)
            v = Pb[NA + k, t, r, pl.ds(0, FW)].astype(F32) + d_back[k, q].astype(F32)
            Pb[NA + k, t, r, pl.ds(0, FW)] = v.astype(BF)

    def a_route(g):
        def src(q):
            r = pl.ds(pl.multiple_of(q // 4 * 16, 16), 16)
            c = pl.ds(pl.multiple_of(lax.rem(q, 4) * 256, 256), 256)
            return S1.at[pl.ds(g * NG, NG), r, c]

        a = 2 * (ND + g)
        owns[a] = exchange(a, src, a_in.at[g])

    def a_return(g):
        a = 2 * (ND + g)
        owns[a].wait()
        all_in(a, a_in.at[g])
        chain(a_in.at[g], a_mid.at[g], CA)
        owns[a + 1] = exchange(a + 1, lambda q: a_mid.at[g, q], a_back.at[g])

    def a_ready(g):
        a = 2 * (ND + g) + 1
        owns[a].wait()
        all_in(a, a_back.at[g])

    def sums(j, b, col):
        u = unit(j, 0)
        r = pl.ds(pl.multiple_of(b * 16, 16), 16)
        v = Pb[j, d, r, col].astype(F32)
        return v + H2[0, u, r, col].astype(F32) + H2[1, u, r, col].astype(F32)

    def finish(j, b, col, v):
        w = v * v
        acc[:, col] += w[0:8] + w[8:16]
        T[j, pl.ds(pl.multiple_of(b * 16, 16), 16), col] = v.astype(BF)

    def pre(j):
        arrived(unit(j, 0))

        @pl.loop(0, CH // 16)
        def _(b):
            CD[j * 8 + b] = sums(j, b, pl.ds(0, FW))

    def fin(j):
        @pl.loop(0, CH // 16)
        def _(b):
            for c in range(4):
                col = pl.ds(c * 256, 256)
                v = CD[j * 8 + b, :, col] + a_back[j // NG, b * 4 + c, j % NG].astype(F32)
                finish(j, b, col, v)

        out_copy(j).start()

    def total(j):
        arrived(unit(j, 0))

        @pl.loop(0, CH // 16)
        def _(b):
            for c in range(4):
                col = pl.ds(c * 256, 256)
                finish(j, b, col, sums(j, b, col))

        out_copy(j).start()

    def out_copy(j):
        return pltpu.make_async_copy(
            T.at[j], out_ref.at[pl.ds(j * CH, CH), :], out_sem.at[j]
        )

    acc[...] = jnp.zeros_like(acc)
    mask(1)
    src0 = functools.partial(d_src, 0)
    route0 = functools.partial(one, 0, src0, d_in.at[0])
    prefetch(2)
    x_wait(0)
    pl.loop(0, 2)(functools.partial(half, 0))
    greet_near()
    for k in range(1, 4):
        route0(at(k, 0, 0))
        route0(at(0, k, 0))
    route0(at(0, 0, 1))
    prefetch(3)
    x_wait(1)
    half(1, 0)
    raw_left(0, 1)
    greet_plane()
    for k in range(1, 4):
        for m in range(1, 4):
            route0(at(k, m, 0))
        route0(at(0, k, 1))
    half(1, 1)
    raw_right(0, 1)
    plane_ready()
    for k in range(1, 4):
        for m in range(4):
            route0(at(k, m, 1))
    owns[0] = keep_own(0, src0, d_in.at[0])

    actions = {
        "c": compute, "h": first_hop, "w": whole_hop, "m": merge, "dr": d_route, "dret": d_return,
        "da": d_add, "r": reduce_second, "ar": a_route, "aret": a_return,
        "ardy": a_ready, "pre": pre, "fin": fin, "tot": total,
    }
    for op in ORDER:
        name = op.rstrip("0123456789")
        if op == "c00":
            mask(0)
        if op == "dret0":
            tab.wait()
        actions[name](*[int(c) for c in op[len(name):]])

    square = jnp.sum(acc[...])
    threshold = limit_ref[0] * math.sqrt(DW * FW)
    upper = lax.broadcasted_iota(jnp.int32, (8, 128), 0) < 4
    norm[...] = jnp.where(upper, square, threshold)
    for k in range(1, DP):
        pltpu.make_async_remote_copy(
            norm, norm_ref.at[d], n_send, n_recv,
            device_id=(lax.rem(d + k, DP), e), device_id_type=MESH,
        ).start()
    mine = pltpu.make_async_copy(norm, norm_ref.at[d], n_own)
    mine.start()

    for u in range(NU):
        pltpu.make_async_copy(
            H2.at[0, pl.ds(0, 3)], H2.at[0, pl.ds(0, 3)], y_send.at[u]
        ).wait()
    for a in range(2 * ND + 4):
        ref = d_in.at[0] if a < 2 * ND else a_in.at[0]
        pltpu.make_async_copy(
            ref.at[pl.ds(0, EX - 1)], ref.at[pl.ds(0, EX - 1)], a2a_send.at[a]
        ).wait()
    for j in range(NJ):
        out_copy(j).wait()
    mine.wait()
    three = norm_ref.at[pl.ds(0, 3)]
    pltpu.make_async_copy(three, three, n_send).wait()
    pltpu.make_async_copy(three, three, n_recv).wait()


def scale(total_ref, norm_ref, out_ref, buf, norm, in_sem, out_sem, norm_sem):
    rows = DW // DP // PARTS
    norm_in = pltpu.make_async_copy(norm_ref, norm, norm_sem)
    ins, outs = [], []
    for i in range(PARTS):
        r = pl.ds(i * rows, rows)
        ins.append(pltpu.make_async_copy(total_ref.at[r, :], buf.at[i], in_sem.at[i]))
        outs.append(pltpu.make_async_copy(buf.at[i], out_ref.at[r, :], out_sem.at[i]))
    norm_in.start()
    for copy in ins:
        copy.start()
    norm_in.wait()
    whole = norm[0] + norm[1] + norm[2] + norm[3]
    factor = jnp.minimum(1.0, norm[0, 4:5, 0:1] / jnp.sqrt(whole[0:1, 0:1] + 1e-06))
    for i in range(PARTS):
        ins[i].wait()
        buf[i] = (buf[i].astype(F32) * factor).astype(BF)
        outs[i].start()
    for copy in outs:
        copy.wait()


def local(tokens, grads_out, counts, placement, limits):
    dma = pltpu.SemaphoreType.DMA
    total, norms = pl.pallas_call(
        body,
        out_shape=(
            jax.ShapeDtypeStruct((DW // DP, FW), BF),
            jax.ShapeDtypeStruct((DP, 8, 128), F32),
        ),
        in_specs=[
            pl.BlockSpec(memory_space=pl.ANY),
            pl.BlockSpec(memory_space=pl.ANY),
            pl.BlockSpec(memory_space=pltpu.SMEM),
            pl.BlockSpec(memory_space=pltpu.VMEM),
            pl.BlockSpec(memory_space=pltpu.SMEM),
        ],
        out_specs=(
            pl.BlockSpec(memory_space=pl.ANY),
            pl.BlockSpec(memory_space=pl.ANY),
        ),
        scratch_shapes=[
            pltpu.VMEM((NX, ROWS, 4 * CH), BF),
            pltpu.VMEM((ROWS, 2 * FW), BF),
            pltpu.VMEM((NJ, 4, CH, 2 * FW), BF),
            pltpu.VMEM((2, NU, CH, HW), BF),
            pltpu.VMEM((2, NU, CH, FW), BF),
            pltpu.VMEM((ND, EX, 16, FW), BF),
            pltpu.VMEM((ND, EX, 16, FW), BF),
            pltpu.VMEM((ND, EX, 16, FW), BF),
            pltpu.VMEM((NA, CH, FW), BF),
            pltpu.VMEM((2, EX, NG, 16, 256), BF),
            pltpu.VMEM((2, EX, NG, 16, 256), BF),
            pltpu.VMEM((2, EX, NG, 16, 256), BF),
            pltpu.VMEM((EX + 1, 16, FW), F32),
            pltpu.VMEM((EX + 1, NG, 16, 256), F32),
            pltpu.VMEM((NJ, CH, FW), BF),
            pltpu.VMEM((8, FW), F32),
            pltpu.VMEM((8, 128), F32),
            pltpu.VMEM((8, 128), jnp.int32),
            pltpu.SMEM((8, 128), jnp.int32),
            pltpu.SemaphoreType.REGULAR,
            pltpu.SemaphoreType.REGULAR,
            dma((NX * 4,)),
            dma((8,)),
            dma,
            dma((NU,)),
            dma((2, NU)),
            dma((2, NU)),
            dma((2 * ND + 4,)),
            dma((2 * ND + 4,)),
            dma((2 * ND + 4,)),
            dma,
            dma,
            dma,
            dma((NJ,)),
        ],
        compiler_params=pltpu.CompilerParams(
            collective_id=0, has_side_effects=True, vmem_limit_bytes=62 * 2**20
        ),
        cost_estimate=pl.CostEstimate(
            flops=4 * ROWS * DW * FW, bytes_accessed=40 * 2**20, transcendentals=0
        ),
    )(tokens, grads_out, counts, placement.reshape(1, EX), limits)
    any_space = pl.BlockSpec(memory_space=pl.ANY)
    out = pl.pallas_call(
        scale,
        out_shape=jax.ShapeDtypeStruct((DW // DP, FW), BF),
        in_specs=[any_space, any_space],
        out_specs=any_space,
        scratch_shapes=[
            pltpu.VMEM((PARTS, DW // DP // PARTS, FW), BF),
            pltpu.VMEM((DP, 8, 128), F32),
            dma((PARTS,)),
            dma((PARTS,)),
            dma,
        ],
    )(total, norms)
    return out[None]


def solution(mesh):
    in_specs = (
        P(("dp", "expert"), None),
        P(("dp", "expert"), None),
        P(("dp", "expert"), None),
        P(),
        P("expert"),
    )
    out_specs = P("expert", "dp", None)
    return jax.shard_map(local, mesh=mesh, in_specs=in_specs, out_specs=out_specs, check_vma=False)
```

time: 124 us -> 113 us (0.911)
  Pallas kernels: 118 us -> 112 us
  other arithmetic: 3.85 us -> 0 us
  local copies, waits for them, and re-layouts: 1.26 us -> 0 us
    pallas_call x1, Pallas kernels: 118 us -> 109 us  [local(): pl.pallas_call(body, out_shape=(jax.ShapeDtypeStruct((DW // DP, FW), BF),...]
    broadcast_in_dim x1 -> x0, other arithmetic: 3.85 us -> none  [local(): return (total.astype(F32) * factor[0, 0]).astype(BF)[None]]
    pallas_call x0 -> x1, Pallas kernels: none -> 2.65 us  [local(): pl.pallas_call(scale, out_shape=jax.ShapeDtypeStruct((DW // DP, FW), BF),...]
    slice x1 -> x0, local copies, waits for them, and re-layouts: 1.26 us -> none  [local(): return (total.astype(F32) * factor[0, 0]).astype(BF)[None]]
where the time goes in v2:
time: 113 us
  Pallas kernels  112 us (99%)
    pallas_call x1, Pallas kernels, local(): pl.pallas_call(body, out_shape=(jax.ShapeDtypeStruct((DW // DP, FW), BF),...  109 us
    pallas_call x1, Pallas kernels, local(): pl.pallas_call(scale, out_shape=jax.ShapeDtypeStruct((DW // DP, FW), BF),...  2.65 us

profile of v2, /device:TPU:0, one launch (start us, length us, event | category | flops | bytes accessed | tf_op | source)
XLA Modules:
  0.0 112.8 jit_solution(17944433133785159218)
XLA Ops:
  0.7 109.3 %shard_map.55 = (bf16[896,1024]{1,0:T(8,128)(2,1)}, f32[4,8,128]{2,1,0:T(8,128)}) custom-call(bf16[2048,3584]{1,0:T(8,128)(2,1)} %x_ref.1, bf16[2048,1024]{1,0:T(8,128)(2,1)} %g_ref.1, s32[1,2]{1,0:T(1,128)} %counts_ref.1, s32[1,32]{1,0:T(1,128)} %bitcast.2, f32[1]{0:T(128)S(6)} %copy.6.limit_ref), custom_call_target="tpu_custom_call" | custom-call | flops 30064771072 | bytes 41943040 | tf_op jit(solution)/shard_map/pallas_call | solution.py:470
  110.0 2.6 %shard_map.56 = bf16[896,1024]{1,0:T(8,128)(2,1)} custom-call(bf16[896,1024]{1,0:T(8,128)(2,1)} %get-tuple-element.7.total_ref, f32[4,8,128]{2,1,0:T(8,128)} %get-tuple-element.8.norm_ref), custom_call_target="tpu_custom_call" | custom-call | tf_op jit(solution)/shard_map/pallas_call | solution.py:531

commit v3 on v2

--- a/solution.py
+++ b/solution.py
@@ -156,16 +156,16 @@
             for c in x_load(n, steps[n][0]):
                 c.start()
 
-    def half(i, n):
+    def product(i, start, width):
         j, s = steps[i]
-        col = pl.ds(pl.multiple_of(s * FW + n * 512, 512), 512)
+        col = pl.ds(s * FW + start, width)
         r = lax.dot_general(
             xc[i % NX],
             G[:, col],
             (((0,), (0,)), ((), ())),
             preferred_element_type=F32,
         )
-        Pb[j, :, :, col] = r.astype(BF).reshape(4, CH, 512)
+        Pb[j, :, :, col] = r.astype(BF).reshape(4, CH, width)
 
     def x_wait(i):
         for c in x_load(i, steps[i][0]):
@@ -175,7 +175,7 @@
         i = steps.index((j, s))
         prefetch(i + NX - 1)
         x_wait(i)
-        pl.loop(0, 2)(functools.partial(half, i))
+        product(i, 0, FW)
 
     def y_copy(src, dst, u, sem, target):
         return pltpu.make_async_remote_copy(
@@ -378,7 +378,7 @@
     route0 = functools.partial(one, 0, src0, d_in.at[0])
     prefetch(2)
     x_wait(0)
-    pl.loop(0, 2)(functools.partial(half, 0))
+    product(0, 0, FW)
     greet_near()
     for k in range(1, 4):
         route0(at(k, 0, 0))
@@ -386,14 +386,14 @@
     route0(at(0, 0, 1))
     prefetch(3)
     x_wait(1)
-    half(1, 0)
+    product(1, 0, HW)
     raw_left(0, 1)
     greet_plane()
     for k in range(1, 4):
         for m in range(1, 4):
             route0(at(k, m, 0))
         route0(at(0, k, 1))
-    half(1, 1)
+    product(1, HW, HW)
     raw_right(0, 1)
     plane_ready()
     for k in range(1, 4):

time: 113 us -> 113 us (level)
  no operation moved by 1% of the time
where the time goes in v3:
time: 113 us
  Pallas kernels  112 us (99%)
    pallas_call x1, Pallas kernels, local(): pl.pallas_call(body, out_shape=(jax.ShapeDtypeStruct((DW // DP, FW), BF),...  109 us
    pallas_call x1, Pallas kernels, local(): pl.pallas_call(scale, out_shape=jax.ShapeDtypeStruct((DW // DP, FW), BF),...  2.65 us

profile of v3, /device:TPU:0, one launch (start us, length us, event | category | flops | bytes accessed | tf_op | source)
XLA Modules:
  0.0 112.5 jit_solution(9249283734839001194)
XLA Ops:
  0.7 109.1 %shard_map.55 = (bf16[896,1024]{1,0:T(8,128)(2,1)}, f32[4,8,128]{2,1,0:T(8,128)}) custom-call(bf16[2048,3584]{1,0:T(8,128)(2,1)} %x_ref.1, bf16[2048,1024]{1,0:T(8,128)(2,1)} %g_ref.1, s32[1,2]{1,0:T(1,128)} %counts_ref.1, s32[1,32]{1,0:T(1,128)} %bitcast.2, f32[1]{0:T(128)S(6)} %copy.6.limit_ref), custom_call_target="tpu_custom_call" | custom-call | flops 30064771072 | bytes 41943040 | tf_op jit(solution)/shard_map/pallas_call | solution.py:470
  109.7 2.6 %shard_map.56 = bf16[896,1024]{1,0:T(8,128)(2,1)} custom-call(bf16[896,1024]{1,0:T(8,128)(2,1)} %get-tuple-element.7.total_ref, f32[4,8,128]{2,1,0:T(8,128)} %get-tuple-element.8.norm_ref), custom_call_target="tpu_custom_call" | custom-call | tf_op jit(solution)/shard_map/pallas_call | solution.py:531
